TPU v7x, 512 devices: a whole 4x8x8 slice. The times are simulated.
512 devices in a mesh: comp: 128 (over z, y, core), col: 4 (over x).
Axes of the slice: x: 4, y: 8, z: 8, core: 2. Of those that a mesh axis runs over, the one named last changes fastest.
Arguments:
- operators: bfloat16 [1024, 512, 1024], P('comp', 'col'), may hold values from -0.1875 to 0.1875
- excitations: bfloat16 [1024, 1024, 512], P('comp', None, 'col'), may hold values from -6 to 6
- comp_scale: float32 [1024], P('comp'), may hold values from 0.2 to 5
- live_count: int32 [128], P('comp'), may hold values from 1 to 8, 512 in all
- port_of: int32 [1024, 64], P('comp', 'col'), may hold values from 0 to 65535, as said below
Outputs:
- port_basis: bfloat16 [65536, 8, 256], P(('comp', 'col'))
- upper_factor: float32 [512, 512], replicated
Inputs may be any that keep to these rules, and one draw needn't show every extreme that they name: `live_count`: 8 on some comp device in every draw; the entries sum to 512. `port_of`: a permutation of the port block positions; position p belongs to comp device p // 512 and col device (p // 128) % 4, and a block stays on its col device; of the blocks one device holds, exactly 2 go to each of 64 comp devices.
All inputs are finite; a program needn't handle non-finite values.
Results may differ from a plain program's by a relative error of at most 0.0085.
Values may be sent and summed in bfloat16 or wider, within the bound.
A program may use at most 64 MiB of HBM per device.

v0:
```python
import jax
import jax.numpy as jnp
from jax import lax
from jax.sharding import PartitionSpec as P

MODES = 256


def exact_dot(left, right):
    return jnp.dot(left, right, precision=lax.Precision.HIGHEST, preferred_element_type=jnp.float32)


def apply_components(matrices, columns, scales, living):
    initial = jnp.zeros((matrices.shape[0], matrices.shape[1], columns.shape[2]), jnp.bfloat16)

    def advance(which, collected):
        operator_one = lax.dynamic_index_in_dim(matrices, which, 0, keepdims=False)
        excite_one = lax.dynamic_index_in_dim(columns, which, 0, keepdims=False)
        product = (
            jnp.dot(operator_one, excite_one, preferred_element_type=jnp.float32) * scales[which]
        )
        return lax.dynamic_update_index_in_dim(collected, product.astype(jnp.bfloat16), which, 0)

    return lax.fori_loop(0, living, advance, initial)


def routing(port_of, comp_count, col_count):
    flat_port = port_of.reshape(-1)
    per_dev = flat_port.shape[0]
    target = flat_port // (col_count * per_dev)
    place_in = flat_port % per_dev
    indices = jnp.arange(per_dev)
    matching = (target[:, None] == target[None, :]) & (indices[None, :] < indices[:, None])
    position = jnp.sum(matching.astype(jnp.int32), axis=1)
    capacity = 2 * per_dev // comp_count
    return (target, position, place_in, capacity)


def pack_blocks(blocks, route, comp_count):
    target, position, place_in, capacity = route
    per_dev = blocks.shape[0]
    slot_of = target * capacity + position
    slot_ids = jnp.arange(comp_count * capacity, dtype=jnp.int32)
    picking = slot_ids[:, None] == slot_of[None, :]
    flat = blocks.reshape(per_dev, -1)
    outgoing = jnp.dot(
        picking.astype(blocks.dtype), flat, preferred_element_type=jnp.float32
    ).astype(blocks.dtype)
    outgoing = outgoing.reshape((comp_count, capacity) + blocks.shape[1:])
    filled = jnp.sum(picking.astype(jnp.int32), axis=1)
    chosen = jnp.sum(jnp.where(picking, place_in[None, :], 0), axis=1)
    labels = jnp.where(filled > 0, chosen, per_dev).reshape(comp_count, capacity)
    return (outgoing, labels)


def unpack_blocks(incoming, labels, per_dev):
    shaped = incoming.reshape(incoming.shape[0] * incoming.shape[1], -1)
    wanted = jnp.arange(per_dev, dtype=jnp.int32)
    picking = (wanted[:, None] == labels.reshape(-1)[None, :]).astype(incoming.dtype)
    placed = jnp.dot(picking, shaped, preferred_element_type=jnp.float32).astype(incoming.dtype)
    return placed.reshape((per_dev,) + incoming.shape[2:])


def factorize(gram, head):
    lower = jnp.linalg.cholesky(gram)
    head_block = lower[:head, :head]
    identity_block = jnp.eye(head, dtype=jnp.float32)
    head_inverse = jax.scipy.linalg.solve_triangular(head_block, identity_block, lower=True)
    return (lower.T, head_inverse.T)


def port_modes(row_data, solver_table):
    leading = row_data.astype(jnp.float32)
    return exact_dot(leading, solver_table).astype(jnp.bfloat16)


def on_device(operators, excitations, comp_scale, live_count, port_of):
    living = live_count[0]
    whole = apply_components(
        lax.all_gather(operators, "col", axis=1, tiled=True), excitations, comp_scale, living
    )
    snapshot = lax.all_to_all(whole, "col", split_axis=1, concat_axis=2, tiled=True)
    columns_all = snapshot.shape[2]
    row_data = snapshot.reshape(-1, columns_all)
    comp_count = lax.axis_size("comp")
    col_count = lax.axis_size("col")
    route = routing(port_of, comp_count, col_count)
    per_dev = route[0].shape[0]
    outgoing, labels = pack_blocks(
        row_data[:, :MODES].reshape(per_dev, -1, MODES), route, comp_count
    )
    incoming, got_labels = (
        lax.all_to_all(outgoing, "comp", split_axis=0, concat_axis=0, tiled=True),
        lax.all_to_all(labels, "comp", split_axis=0, concat_axis=0, tiled=True),
    )
    arrived = unpack_blocks(incoming, got_labels, per_dev)
    local_gram = lax.dot_general(
        row_data, row_data, (((0,), (0,)), ((), ())), preferred_element_type=jnp.float32
    )
    gram_sum = lax.psum(local_gram, ("comp", "col"))
    total_rows = row_data.shape[0] * comp_count * col_count
    upper_factor, solver_table = factorize(gram_sum / total_rows, MODES)
    port_basis = port_modes(arrived.reshape(-1, arrived.shape[-1]), solver_table).reshape(
        per_dev, -1, MODES
    )
    return (port_basis, upper_factor)


def solution(mesh):
    placed = (
        P("comp", "col", None),
        P("comp", None, "col"),
        P("comp"),
        P("comp"),
        P("comp", "col"),
    )
    return jax.shard_map(
        on_device,
        mesh=mesh,
        in_specs=placed,
        out_specs=(P(("comp", "col"), None, None), P()),
        check_vma=False,
    )
```

profile of v0, /device:TPU:1, one launch (start us, length us, event | category | flops | bytes accessed | tf_op | source)
XLA Modules:
  0.0 574.2 jit_solution(14065416596521578248)
XLA Ops:
  7.9 96.1 %all-gather.2.cloned.1.call-done = bf16[8,512,1024]{2,1,0:T(8,128)(2,1)} async-done(((bf16[8,128,1024]{2,1,0:T(8,128)(2,1)}), bf16[8,512,1024]{2,1,0:T(8,128)(2,1)}) %all-gather.2.cloned.1.call-update) | async-done | bytes 8388624 | tf_op jit(solution)/shard_map/all_gather | solution.py:80
  104.2 8.0 %while.11 = (s32[]{:T(128)}, bf16[8,512,128]{2,1,0:T(8,128)(2,1)S(1)}, s32[]{:T(128)}, bf16[8,512,1024]{2,1,0:T(8,128)(2,1)}, bf16[8,1024,128]{2,1,0:T(8,128)(2,...) while((s32[]{:T(128)}, bf16[8,512,128]{2,1,0:T(8,128)(2,1)S(1)}, s32[]{:T(128)}, ...), condition=%wide.region_4.5_spmd, body=%wide.region_3.4_spmd.sunk | while | flops 134348800 | bytes 1443979 | solution.py:24
  105.5 2.4 fusion.47
  109.1 2.4 fusion.47
  112.2 1.6 copy.27
  113.8 3.7 all-to-all-start.1
  118.0 9.3 %all-to-all-done.1 = bf16[8,512,128]{2,0,1:T(8,128)(2,1)S(1)} async-done(((bf16[8,512,128]{2,0,1:T(8,128)(2,1)}), bf16[8,512,128]{2,0,1:T(8,128)(2,1)S(1)}, u32[]{:S(2)}, u32[]{:S(2)}) %all-to-all-start.1) | async-done | bytes 1048608 | tf_op jit(solution)/shard_map/all_to_all | solution.py:82
  128.2 1.7 fusion.32
  130.8 41.0 %all-to-all-start = ((s32[128,1,2]{2,1,0:T(1,128)}), s32[128,1,2]{2,1,0:T(1,128)S(1)}, u32[]{:S(2)}, u32[]{:S(2)}) async-start(s32[128,1,2]{2,1,0:T(1,128)} %bitcast.4), calls=%async_computation | async-start | bytes 131072 | tf_op jit(solution)/shard_map/all_to_all | solution.py:94
  171.9 11.3 %all-to-all-done = s32[128,1,2]{2,1,0:T(1,128)S(1)} async-done(((s32[128,1,2]{2,1,0:T(1,128)}), s32[128,1,2]{2,1,0:T(1,128)S(1)}, u32[]{:S(2)}, u32[]{:S(2)}) %all-to-all-start) | async-done | bytes 1056 | tf_op jit(solution)/shard_map/all_to_all | solution.py:94
  187.2 6.2 %all-to-all-start.2 = ((bf16[128,2,8,256]{3,2,1,0:T(8,128)(2,1)}), bf16[128,2,8,256]{3,2,1,0:T(8,128)(2,1)S(1)}, u32[]{:S(2)}, u32[]{:S(2)}) async-start(bf16[128,2,8,256]{3,2,1,0:T(8,128)(2,1)} %bitcast.29), calls=%async_computation.2 | async-start | bytes 2097152 | tf_op jit(solution)/shard_map/all_to_all | solution.py:93
  193.4 253.0 %all-reduce.3.cloned.1.call-done = f32[512,512]{0,1:T(8,128)} async-done(((f32[512,512]{0,1:T(8,128)}), f32[512,512]{0,1:T(8,128)}) %all-reduce.3.cloned.1.call-update) | async-done | bytes 1048592 | tf_op jit(solution)/shard_map/psum | solution.py:100
  446.4 2.4 broadcast_multiply_fusion
  448.7 1.6 copy.31
  451.5 11.7 %cholesky.104 = f32[128,128]{1,0:T(8,128)S(1)} custom-call(f32[128,128]{1,0:T(8,128)S(1)} %cholesky.266), custom_call_target="Cholesky" | custom-call | tf_op jit(solution)/shard_map/jit(cholesky)/cholesky | solution.py:65
  463.3 9.8 %custom-call.31 = f32[1,128,128]{1,2,0:T(8,128)S(1)} custom-call(f32[1,128,128]{2,1,0:T(8,128)S(1)} %get-tuple-element.87), custom_call_target="InvertDiagBlocksLowerTriangular" | custom-call | tf_op jit(solution)/shard_map/jit(cholesky)/cholesky | solution.py:65
  475.8 11.7 %cholesky.217 = f32[128,128]{1,0:T(8,128)S(1)} custom-call(f32[128,128]{1,0:T(8,128)S(1)} %cholesky.270), custom_call_target="Cholesky" | custom-call | tf_op jit(solution)/shard_map/jit(cholesky)/cholesky | solution.py:65
  487.5 10.0 %custom-call.32 = f32[1,128,128]{1,2,0:T(8,128)S(1)} custom-call(f32[1,128,128]{2,1,0:T(8,128)S(1)} %get-tuple-element.84), custom_call_target="InvertDiagBlocksLowerTriangular" | custom-call | tf_op jit(solution)/shard_map/jit(cholesky)/cholesky | solution.py:65
  499.0 11.7 %cholesky.238 = f32[128,128]{1,0:T(8,128)S(1)} custom-call(f32[128,128]{1,0:T(8,128)S(1)} %cholesky.275), custom_call_target="Cholesky" | custom-call | tf_op jit(solution)/shard_map/jit(cholesky)/cholesky | solution.py:65
  511.5 9.8 %custom-call.33 = f32[1,128,128]{1,2,0:T(8,128)S(1)} custom-call(f32[1,128,128]{2,1,0:T(8,128)S(1)} %get-tuple-element.81), custom_call_target="InvertDiagBlocksLowerTriangular" | custom-call | tf_op jit(solution)/shard_map/jit(cholesky)/cholesky | solution.py:65
  522.8 11.7 %cholesky.255 = f32[128,128]{1,0:T(8,128)S(1)} custom-call(f32[128,128]{1,0:T(8,128)S(1)} %convolution_subtract_fusion.3), custom_call_target="Cholesky" | custom-call | tf_op jit(solution)/shard_map/jit(cholesky)/cholesky | solution.py:65
  540.2 4.1 while.12
  540.8 1.4 bitcast_dynamic-update-slice_fusion.2
  544.3 19.7 %custom-call.34 = f32[2,128,128]{1,2,0:T(8,128)S(1)} custom-call(f32[2,128,128]{2,1,0:T(8,128)S(1)} %get-tuple-element.43), custom_call_target="InvertDiagBlocksLowerTriangular" | custom-call | tf_op jit(solution)/shard_map/jit(_solve_triangular)/triangular_solve | solution.py:68
  (71 shorter events, 24.7 us)
Async XLA Ops:
  7.2 97.0 %copy-start.3 = (f32[8]{0:T(128)S(1)}, f32[8]{0:T(128)}, u32[]{:S(2)}) copy-start(f32[8]{0:T(128)} %param.9) | copy-start | bytes 100
  7.2 96.9 %all-gather.2.cloned.1.call-start = ((), (), s32[]{:S(2)}) async-start(), calls=%async_computation.3 | async-start | bytes 10485760 | tf_op jit(solution)/shard_map/all_gather | solution.py:80
  112.2 5.4 copy-start.2
  113.8 13.5 %all-to-all-start.1 = ((bf16[8,512,128]{2,0,1:T(8,128)(2,1)}), bf16[8,512,128]{2,0,1:T(8,128)(2,1)S(1)}, u32[]{:S(2)}, u32[]{:S(2)}) async-start(bf16[8,512,128]{2,0,1:T(8,128)(2,1)} %copy.27), calls=%async_computation.1 | async-start | bytes 2097152 | tf_op jit(solution)/shard_map/all_to_all | solution.py:82
  117.6 328.8 %all-reduce.3.cloned.1.call-start = ((), (), s32[]{:S(2)}) async-start(), calls=%async_computation.4 | async-start | bytes 2097152 | tf_op jit(solution)/shard_map/psum | solution.py:100
  130.8 52.4 %all-to-all-start = ((s32[128,1,2]{2,1,0:T(1,128)}), s32[128,1,2]{2,1,0:T(1,128)S(1)}, u32[]{:S(2)}, u32[]{:S(2)}) async-start(s32[128,1,2]{2,1,0:T(1,128)} %bitcast.4), calls=%async_computation | async-start | bytes 131072 | tf_op jit(solution)/shard_map/all_to_all | solution.py:94
  187.2 377.7 %all-to-all-start.2 = ((bf16[128,2,8,256]{3,2,1,0:T(8,128)(2,1)}), bf16[128,2,8,256]{3,2,1,0:T(8,128)(2,1)S(1)}, u32[]{:S(2)}, u32[]{:S(2)}) async-start(bf16[128,2,8,256]{3,2,1,0:T(8,128)(2,1)} %bitcast.29), calls=%async_computation.2 | async-start | bytes 2097152 | tf_op jit(solution)/shard_map/all_to_all | solution.py:93
  446.4 3.9 copy-start
  450.6 1.0 copy-start.1
Sparse Core Ops, SparseCore 0:
  10.1 93.8 all-gather.1
  130.1 316.2 all-reduce.2
where the time goes:
time: 581 us; the launch traced here: 574 us
  waiting for transfers between devices  370 us (64%)
  other arithmetic  103 us (18%)
  starting transfers between devices  51 us (9%)
  between operations  17.2 us (3%)
  local copies, waits for them, and re-layouts  16.1 us (3%)
  matrix products  15 us (3%)
    psum x1, waiting for transfers between devices, on_device(): gram_sum = lax.psum(local_gram, ('comp', 'col'))  253 us
    all_gather x1, waiting for transfers between devices, on_device(): lax.all_gather(operators, 'col', axis=1, tiled=True)  96.1 us
    another operation x14, other arithmetic, factorize(): lower = jnp.linalg.cholesky(gram)  78.8 us
    all_to_all x1, starting transfers between devices, on_device(): lax.all_to_all(labels, 'comp', split_axis=0, concat_axis=0, tiled=True)  41 us
    another operation x3, other arithmetic, factorize(): jax.scipy.linalg.solve_triangular(head_block, identity_block, lower=True)  19.7 us
  transfers between devices with their start and end apart: 5, of which 4 were waited for; matrix products, arithmetic and copies ran while one was open for 21% of the time, Pallas kernels for 0%

commit v1 on v0

v1 whole, which is shorter than its diff:
```python
import jax
import jax.numpy as jnp
from jax import lax
from jax.experimental import pallas as pl
from jax.experimental.pallas import tpu as pltpu
from jax.sharding import PartitionSpec as P

MESH = pl.DeviceIdType.MESH
NX, NY, NZ, NT = 4, 8, 8, 16
F32, BF16, I32 = jnp.float32, jnp.bfloat16, jnp.int32
FIRST = [(0, 0), (0, 1), (0, 2), (0, 3), (1, 1), (1, 2), (1, 3)]
SECOND = [(2, 2), (2, 3), (3, 3)]


def iota(shape, dim):
    return lax.broadcasted_iota(I32, shape, dim)


def gather_kernel(ops, exc, scale, live, ports, gram_out, lead_out,
                  A, E, W, lead, P_pack, P_un, pmine, pz, ptile, pall,
                  PA, PB, RA1, RA2, RB1, RB2,
                  g0, g1, r0c, r1c, s0, s1, rz0, ry1, t0, t1, ry0, rz1, u0, u1, rx0, rx1,
                  ay0, az1, az0, ay1, f0, f1,
                  local_sem, s_ops, r_ops, s_exc, r_exc, s_pz, r_pz, s_py, r_py, s_ld, r_ld,
                  s_core, r_core, s_red, r_red, s_x, r_x, s_rel, r_rel):
    comp, x = lax.axis_index("comp"), lax.axis_index("col")
    z, y, core = comp // 16, (comp // 2) % 8, comp % 2
    t = y * 2 + core

    def at(xx=None, yy=None, zz=None, cc=None):
        xx, yy, zz, cc = (x if xx is None else xx, y if yy is None else yy, z if zz is None else zz, core if cc is None else cc)
        return ((zz * 8 + yy) * 2 + cc, xx)

    def at_t(tt):
        return (z * 16 + tt, x)

    started = []

    def send(src, dst, ss, rs, to):
        copy = pltpu.make_async_remote_copy(src_ref=src, dst_ref=dst, send_sem=ss, recv_sem=rs, device_id=to, device_id_type=MESH)
        copy.start()
        started.append(copy)

    def arrived(dst, ss, rs, frm):
        pltpu.make_async_remote_copy(src_ref=dst, dst_ref=dst, send_sem=ss, recv_sem=rs, device_id=frm, device_id_type=MESH).wait_recv()

    xs = [(d, lax.rem(x + d, NX), lax.rem(x + NX - d, NX)) for d in (1, 3, 2)]
    ys = [(d, lax.rem(y + d, NY), lax.rem(y + NY - d, NY)) for d in (4, 3, 5, 2, 6, 1, 7)]
    zs = [(d, lax.rem(z + d, NZ), lax.rem(z + NZ - d, NZ)) for d in (4, 3, 5, 2, 6, 1, 7)]
    ts = [(d, lax.rem(t + d, NT), lax.rem(t + NT - d, NT)) for d in (8, 7, 9, 6, 10, 5, 11, 4, 12, 3, 13, 2, 14, 1, 15)]
    other = 1 - core

    barrier = pltpu.get_barrier_semaphore()
    for _, to, _ in xs:
        pl.semaphore_signal(barrier, inc=1, device_id=at(xx=to), device_id_type=MESH)
    for _, to, _ in zs:
        pl.semaphore_signal(barrier, inc=1, device_id=at(zz=to), device_id_type=MESH)
    for _, to, _ in ts:
        pl.semaphore_signal(barrier, inc=1, device_id=at_t(to), device_id_type=MESH)

    own = []
    for k in range(2):
        own.append(pltpu.make_async_copy(ops.at[2 * x + k], A.at[k, pl.ds(pl.multiple_of(x * 128, 128), 128), :], local_sem.at[k]))
        own.append(pltpu.make_async_copy(exc.at[2 * x + k], E.at[k, :, pl.ds(pl.multiple_of(x * 128, 128), 128)], local_sem.at[2 + k]))
    for copy in own:
        copy.start()
    pl.semaphore_wait(barrier, 3 + 7 + 15)

    rows_me = pl.ds(pl.multiple_of(x * 128, 128), 128)
    for k in range(2):
        for d, to, _ in xs:
            send(ops.at[2 * to + k], A.at[k, rows_me, :], s_ops.at[k, d - 1], r_ops.at[k, d - 1], at(xx=to))
            send(exc.at[2 * to + k], E.at[k, :, rows_me], s_exc.at[k, d - 1], r_exc.at[k, d - 1], at(xx=to))

    p_local = ports[...]
    pmine[...] = jnp.broadcast_to(p_local, (8, 128)).astype(F32)
    pz[z] = pmine[...]
    for d, to, _ in zs:
        send(pmine, pz.at[z], s_pz.at[d - 1], r_pz.at[d - 1], at(zz=to))
    target = p_local // 512
    target_all = jnp.broadcast_to(target.astype(F32), (128, 128))
    target_col = target_all.T
    earlier = (target_col == target_all) & (iota((128, 128), 0) < iota((128, 128), 1))
    rank = jnp.sum(earlier.astype(F32), axis=0, keepdims=True)
    base = jnp.broadcast_to(target.astype(F32) * 2 + rank, (8, 128)).astype(BF16)
    spread = (iota((128, 1024), 1) // 8 == iota((128, 1024), 0)).astype(BF16)
    key = jnp.dot(base, spread, preferred_element_type=F32)[0:1, :].astype(I32) * 8 + iota((1, 1024), 1) % 8

    def fill_pack(n, carry):
        P_pack[pl.ds(pl.multiple_of(n * 128, 128), 128), :] = (iota((128, 1024), 0) + n * 128 == key).astype(F32).astype(BF16)
        return carry
    lax.fori_loop(0, 16, fill_pack, 0)

    for d, _, frm in zs:
        arrived(pz.at[frm], s_pz.at[d - 1], r_pz.at[d - 1], at(zz=frm))
    tile = jnp.concatenate([pz[n, 0:1, :] for n in range(8)], axis=0)
    ptile[...] = tile
    pall[t] = tile
    for d, to, _ in ts:
        send(ptile, pall.at[t], s_py.at[d - 1], r_py.at[d - 1], at_t(to))
    for d, _, frm in ts:
        arrived(pall.at[frm], s_py.at[d - 1], r_py.at[d - 1], at_t(frm))
    every = pall[...].reshape(128, 128).astype(I32)
    mine = jnp.where(every // 512 == comp, every % 128 + 1, 0).astype(F32).T
    is_mine = (mine > 0.5)
    below = (iota((128, 128), 1) < iota((128, 128), 0)).astype(BF16)
    order = jnp.dot(below, is_mine.astype(F32).astype(BF16), preferred_element_type=F32)
    zero = jnp.zeros((128, 128), F32)
    first = jnp.sum(jnp.where(is_mine & (order < 0.5), mine, zero), axis=0, keepdims=True)
    second = jnp.sum(jnp.where(is_mine & (order > 0.5), mine, zero), axis=0, keepdims=True)
    both = jnp.concatenate([first, second, jnp.zeros((6, 128), F32)], axis=0).astype(BF16)
    lane = iota((128, 2048), 1) // 16
    widen = ((lane % 16) * 8 + lane // 16 == iota((128, 2048), 0)).astype(F32).astype(BF16)
    wide = jnp.dot(both, widen, preferred_element_type=F32)
    which = (iota((1, 2048), 1) // 8) % 2
    place = jnp.where(which == 0, wide[0:1, :], wide[1:2, :]).astype(I32) * 8 - 8 + iota((1, 2048), 1) % 8

    def fill_un(n, carry):
        P_un[pl.ds(pl.multiple_of(n * 128, 128), 128), :] = (iota((128, 2048), 0) + n * 128 == place).astype(F32).astype(BF16)
        return carry
    lax.fori_loop(0, 8, fill_un, 0)

    for copy in own:
        copy.wait()
    gram = jnp.zeros((512, 512), F32)
    for k in range(2):
        for d, _, frm in xs:
            there = pl.ds(pl.multiple_of(frm * 128, 128), 128)
            arrived(A.at[k, there, :], s_ops.at[k, d - 1], r_ops.at[k, d - 1], at(xx=frm))
            arrived(E.at[k, :, there], s_exc.at[k, d - 1], r_exc.at[k, d - 1], at(xx=frm))
        slot = 2 * x + k
        alive = jnp.minimum(jnp.maximum(live[0] - slot, 0), 1).astype(F32)
        weight = scale[slot] * alive

        def rows(n, carry):
            where = pl.ds(pl.multiple_of(n * 128, 128), 128)
            product = jnp.dot(A[k, where, :], E[k], preferred_element_type=F32)
            W[k, where, :] = (product * weight).astype(BF16)
            return carry
        lax.fori_loop(0, 4, rows, 0)
        for d, to, _ in xs:
            send(W.at[k, pl.ds(pl.multiple_of(to * 128, 128), 128), pl.ds(0, 256)], lead.at[2 * x + k], s_ld.at[k, d - 1], r_ld.at[k, d - 1], at(xx=to))
        lead[2 * x + k] = W[k, rows_me, 0:256]

    def gram_block(r, c):
        out = lax.dot_general(W[0, :, r * 128:(r + 1) * 128], W[0, :, c * 128:(c + 1) * 128], (((0,), (0,)), ((), ())), preferred_element_type=F32)
        return out + lax.dot_general(W[1, :, r * 128:(r + 1) * 128], W[1, :, c * 128:(c + 1) * 128], (((0,), (0,)), ((), ())), preferred_element_type=F32)

    for n, (r, c) in enumerate(FIRST):
        g0[n * 128:(n + 1) * 128, :] = gram_block(r, c)
    for n, (r, c) in enumerate(SECOND):
        g1[n * 128:(n + 1) * 128, :] = gram_block(r, c)

    send(g0.at[pl.ds(pl.multiple_of(other * 448, 64), 448), :], r0c, s_core.at[0], r_core.at[0], at(cc=other))
    send(g1.at[pl.ds(pl.multiple_of(other * 192, 64), 192), :], r1c, s_core.at[1], r_core.at[1], at(cc=other))
    arrived(r0c, s_core.at[0], r_core.at[0], at(cc=other))
    s0[...] = g0[pl.ds(pl.multiple_of(core * 448, 64), 448), :] + r0c[...]
    for d, to, _ in zs:
        send(s0.at[pl.ds(pl.multiple_of(to * 56, 8), 56), :], rz0.at[z], s_red.at[0, d - 1], r_red.at[0, d - 1], at(zz=to))
    arrived(r1c, s_core.at[1], r_core.at[1], at(cc=other))
    s1[...] = g1[pl.ds(pl.multiple_of(core * 192, 64), 192), :] + r1c[...]
    for d, to, _ in ys:
        send(s1.at[pl.ds(pl.multiple_of(to * 24, 8), 24), :], ry1.at[y], s_red.at[1, d - 1], r_red.at[1, d - 1], at(yy=to))
    rz0[z] = s0[pl.ds(pl.multiple_of(z * 56, 8), 56), :]
    ry1[y] = s1[pl.ds(pl.multiple_of(y * 24, 8), 24), :]

    for k in range(2):
        for d, _, frm in xs:
            arrived(lead.at[2 * frm + k], s_ld.at[k, d - 1], r_ld.at[k, d - 1], at(xx=frm))

    def pack(n, carry):
        packed = jnp.dot(P_pack[pl.ds(pl.multiple_of(n * 256, 256), 256), :], lead[...].reshape(1024, 256), preferred_element_type=F32).astype(BF16)
        PA[pl.ds(n * 16, 16)] = packed[:, 0:128].reshape(16, 16, 128)
        PB[n] = packed[:, 128:256].reshape(16, 16, 128)
        return carry
    lax.fori_loop(0, 8, pack, 0)
    for (d, to, _) in zs:
        send(PA.at[pl.ds(to * 16, 16)], RA1.at[z], s_rel.at[0, d - 1], r_rel.at[0, d - 1], at(zz=to))
    for (d, to, _) in ts:
        send(PB.at[:, to], RB1.at[t], s_rel.at[1, d - 1], r_rel.at[1, d - 1], at_t(to))
    RA1[z] = PA[pl.ds(z * 16, 16)]
    RB1[t] = PB[:, t]

    for d, _, frm in zs:
        arrived(rz0.at[frm], s_red.at[0, d - 1], r_red.at[0, d - 1], at(zz=frm))
    t0[0:56, :] = sum([rz0[n] for n in range(1, 8)], rz0[0])
    t0[56:64, :] = jnp.zeros((8, 128), F32)
    for d, to, _ in ys:
        send(t0.at[pl.ds(pl.multiple_of(to * 8, 8), 8), :], ry0.at[y], s_red.at[2, d - 1], r_red.at[2, d - 1], at(yy=to))
    ry0[y] = t0[pl.ds(pl.multiple_of(y * 8, 8), 8), :]
    for d, _, frm in ys:
        arrived(ry1.at[frm], s_red.at[1, d - 1], r_red.at[1, d - 1], at(yy=frm))
    t1[0:24, :] = sum([ry1[n] for n in range(1, 8)], ry1[0])
    t1[24:64, :] = jnp.zeros((40, 128), F32)
    for d, to, _ in zs:
        send(t1.at[pl.ds(pl.multiple_of(to * 8, 8), 8), :], rz1.at[z], s_red.at[3, d - 1], r_red.at[3, d - 1], at(zz=to))
    rz1[z] = t1[pl.ds(pl.multiple_of(z * 8, 8), 8), :]

    for d, _, frm in ys:
        arrived(ry0.at[frm], s_red.at[2, d - 1], r_red.at[2, d - 1], at(yy=frm))
    u0[...] = sum([ry0[n] for n in range(1, 8)], ry0[0])
    for d, to, _ in xs:
        send(u0, rx0.at[x], s_x.at[0, d - 1], r_x.at[0, d - 1], at(xx=to))
    rx0[x] = u0[...]
    for d, _, frm in zs:
        arrived(rz1.at[frm], s_red.at[3, d - 1], r_red.at[3, d - 1], at(zz=frm))
    u1[...] = sum([rz1[n] for n in range(1, 8)], rz1[0])
    for d, to, _ in xs:
        send(u1, rx1.at[x], s_x.at[1, d - 1], r_x.at[1, d - 1], at(xx=to))
    rx1[x] = u1[...]

    for d, _, frm in xs:
        arrived(rx0.at[frm], s_x.at[0, d - 1], r_x.at[0, d - 1], at(xx=frm))
    ay0[pl.ds(pl.multiple_of(y * 8, 8), 8), :] = (rx0[0] + rx0[1]) + (rx0[2] + rx0[3])
    mine0 = ay0.at[pl.ds(pl.multiple_of(y * 8, 8), 8), :]
    for d, to, _ in ys:
        send(mine0, mine0, s_red.at[4, d - 1], r_red.at[4, d - 1], at(yy=to))
    for d, _, frm in xs:
        arrived(rx1.at[frm], s_x.at[1, d - 1], r_x.at[1, d - 1], at(xx=frm))
    az1[pl.ds(pl.multiple_of(z * 8, 8), 8), :] = (rx1[0] + rx1[1]) + (rx1[2] + rx1[3])
    mine1 = az1.at[pl.ds(pl.multiple_of(z * 8, 8), 8), :]
    for d, to, _ in zs:
        send(mine1, mine1, s_red.at[5, d - 1], r_red.at[5, d - 1], at(zz=to))

    for d, _, frm in ys:
        arrived(ay0.at[pl.ds(pl.multiple_of(frm * 8, 8), 8), :], s_red.at[4, d - 1], r_red.at[4, d - 1], at(yy=frm))
    az0[z] = ay0[0:56, :]
    for d, to, _ in zs:
        send(ay0.at[0:56, :], az0.at[z], s_red.at[6, d - 1], r_red.at[6, d - 1], at(zz=to))
    for d, _, frm in zs:
        arrived(az1.at[pl.ds(pl.multiple_of(frm * 8, 8), 8), :], s_red.at[5, d - 1], r_red.at[5, d - 1], at(zz=frm))
    ay1[y] = az1[0:24, :]
    for d, to, _ in ys:
        send(az1.at[0:24, :], ay1.at[y], s_red.at[7, d - 1], r_red.at[7, d - 1], at(yy=to))

    for d, _, frm in zs:
        arrived(RA1.at[frm], s_rel.at[0, d - 1], r_rel.at[0, d - 1], at(zz=frm))
    for d, to, _ in ts:
        send(RA1.at[:, to], RA2.at[:, t], s_rel.at[2, d - 1], r_rel.at[2, d - 1], at_t(to))
    RA2[:, t] = RA1[:, t]
    for d, _, frm in ts:
        arrived(RB1.at[frm], s_rel.at[1, d - 1], r_rel.at[1, d - 1], at_t(frm))
    for d, to, _ in zs:
        send(RB1.at[:, to], RB2.at[z], s_rel.at[3, d - 1], r_rel.at[3, d - 1], at(zz=to))
    RB2[z] = RB1[:, z]

    for d, _, frm in zs:
        arrived(az0.at[frm], s_red.at[6, d - 1], r_red.at[6, d - 1], at(zz=frm))
    f0[core] = az0[...].reshape(448, 128)
    mine_f0 = f0.at[core]
    send(mine_f0, mine_f0, s_core.at[2], r_core.at[2], at(cc=other))
    for d, _, frm in ys:
        arrived(ay1.at[frm], s_red.at[7, d - 1], r_red.at[7, d - 1], at(yy=frm))
    f1[core] = ay1[...].reshape(192, 128)
    mine_f1 = f1.at[core]
    send(mine_f1, mine_f1, s_core.at[3], r_core.at[3], at(cc=other))

    for d, _, frm in ts:
        arrived(RA2.at[:, frm], s_rel.at[2, d - 1], r_rel.at[2, d - 1], at_t(frm))
    for d, _, frm in zs:
        arrived(RB2.at[frm], s_rel.at[3, d - 1], r_rel.at[3, d - 1], at(zz=frm))

    def unpack(n, carry):
        where = pl.ds(pl.multiple_of(n * 256, 256), 256)
        pick = P_un[where, :]
        lead_out[where, 0:128] = jnp.dot(pick, RA2[...].reshape(2048, 128), preferred_element_type=F32).astype(BF16)
        lead_out[where, 128:256] = jnp.dot(pick, RB2[...].reshape(2048, 128), preferred_element_type=F32).astype(BF16)
        return carry
    lax.fori_loop(0, 4, unpack, 0)

    arrived(f0.at[other], s_core.at[2], r_core.at[2], at(cc=other))
    arrived(f1.at[other], s_core.at[3], r_core.at[3], at(cc=other))
    gram_out[0:7] = f0[...].reshape(7, 128, 128)
    gram_out[7:10] = f1[...].reshape(3, 128, 128)
    for copy in started:
        copy.wait_send()


def gather_and_sum(ops, exc, scale, live, ports):
    D = pltpu.SemaphoreType.DMA
    vm = pltpu.VMEM
    V, H, S = (pl.BlockSpec(memory_space=m) for m in (pltpu.VMEM, pl.ANY, pltpu.SMEM))
    scratch = [
        vm((2, 512, 1024), BF16), vm((2, 1024, 512), BF16), vm((2, 512, 512), BF16), vm((8, 128, 256), BF16),
        vm((2048, 1024), BF16), vm((1024, 2048), BF16),
        vm((8, 128), F32), vm((8, 8, 128), F32), vm((8, 128), F32), vm((16, 8, 128), F32),
        vm((128, 16, 128), BF16), vm((8, 16, 16, 128), BF16),
        vm((8, 16, 16, 128), BF16), vm((8, 16, 16, 128), BF16), vm((16, 8, 16, 128), BF16), vm((8, 16, 16, 128), BF16),
        vm((896, 128), F32), vm((384, 128), F32), vm((448, 128), F32), vm((192, 128), F32),
        vm((448, 128), F32), vm((192, 128), F32),
        vm((8, 56, 128), F32), vm((8, 24, 128), F32), vm((64, 128), F32), vm((64, 128), F32),
        vm((8, 8, 128), F32), vm((8, 8, 128), F32), vm((8, 128), F32), vm((8, 128), F32),
        vm((4, 8, 128), F32), vm((4, 8, 128), F32),
        vm((64, 128), F32), vm((64, 128), F32), vm((8, 56, 128), F32), vm((8, 24, 128), F32),
        vm((2, 448, 128), F32), vm((2, 192, 128), F32),
        D((4,)), D((2, 3)), D((2, 3)), D((2, 3)), D((2, 3)), D((7,)), D((7,)), D((15,)), D((15,)), D((2, 3)), D((2, 3)),
        D((4,)), D((4,)), D((8, 7)), D((8, 7)), D((2, 3)), D((2, 3)), D((4, 15)), D((4, 15)),
    ]
    return pl.pallas_call(
        gather_kernel,
        out_shape=(jax.ShapeDtypeStruct((10, 128, 128), F32), jax.ShapeDtypeStruct((1024, 256), BF16)),
        in_specs=[H, H, S, S, V], out_specs=(V, V),
        scratch_shapes=scratch,
        compiler_params=pltpu.CompilerParams(collective_id=0, has_side_effects=True, vmem_limit_bytes=48 << 20),
        name="gather_and_sum",
    )(ops, exc, scale, live, ports)


HI = lax.Precision.HIGHEST

def dot_hi(a, b, ta=False):
    dims = (((0,), (0,)), ((), ())) if ta else (((1,), (0,)), ((), ()))
    return lax.dot_general(a, b, dims, precision=HI, preferred_element_type=jnp.float32)

def factor_block(S):
    sub = lax.broadcasted_iota(jnp.int32, (8, 128), 0)
    lane = lax.broadcasted_iota(jnp.int32, (8, 128), 1)
    S = list(S)
    T = [(lane == sub + 8 * i).astype(jnp.float32) for i in range(16)]
    for j in range(16):
        B = {i: [jnp.broadcast_to(S[i][:, 8 * j + k:8 * j + k + 1], (8, 128)) for k in range(8)] for i in range(j, 16)}
        scale = jnp.zeros((8, 128), jnp.float32)
        for k in range(8):
            piv = B[j][k][k:k + 1, :]
            inv = 1.0 / piv
            scale = jnp.where(sub == k, lax.rsqrt(piv), scale)
            prow, qrow = S[j][k:k + 1, :], T[j][k:k + 1, :]
            brow = [B[j][kk][k:k + 1, :] for kk in range(8)]
            for i in range(j, 16):
                m = B[i][k] * inv
                if i == j:
                    m = jnp.where(sub > k, m, 0.0)
                if i > j or k < 7:
                    S[i] = S[i] - m * prow
                    T[i] = T[i] - m * qrow
                    for kk in range(k + 1, 8):
                        B[i][kk] = B[i][kk] - m * brow[kk]
        S[j] = jnp.where(lane >= sub + 8 * j, S[j], 0.0) * scale
        T[j] = T[j] * scale
    return S, T

def k2_body(g_ref, lead_ref, basis_ref, upper_ref, S, T):
    blocks = [(0, 0), (0, 1), (0, 2), (0, 3), (1, 1), (1, 2), (1, 3), (2, 2), (2, 3), (3, 3)]
    inv_rows = 1.0 / 524288
    for n, (r, c) in enumerate(blocks):
        S[r * 128:(r + 1) * 128, c * 128:(c + 1) * 128] = g_ref[n] * inv_rows
    for r in range(4):
        for c in range(r):
            S[r * 128:(r + 1) * 128, c * 128:(c + 1) * 128] = jnp.zeros((128, 128), jnp.float32)

    def step(kb, carry):
        r0 = pl.multiple_of(kb * 128, 128)
        tiles = [S[pl.ds(r0 + 8 * i, 8), pl.ds(r0, 128)] for i in range(16)]
        U, Tt = factor_block(tiles)
        for i in range(16):
            T[kb, 8 * i:8 * i + 8, :] = Tt[i]
        row = dot_hi(T[kb], S[pl.ds(r0, 128), :])
        col = lax.broadcasted_iota(jnp.int32, (128, 512), 1)
        row = jnp.where(col >= r0 + 128, row, 0.0)
        upper_ref[pl.ds(r0, 128), :] = row
        for i in range(16):
            upper_ref[pl.ds(r0 + 8 * i, 8), pl.ds(r0, 128)] = U[i]
        S[...] = S[...] - dot_hi(row, row, ta=True)
        return carry
    lax.fori_loop(0, 4, step, 0)
    t0, t1 = T[0].T, T[1].T
    cross = -dot_hi(t0, dot_hi(upper_ref[0:128, 128:256], t1))
    top = jnp.concatenate([t0, cross], axis=1)
    bot = jnp.concatenate([jnp.zeros((128, 128), jnp.float32), t1], axis=1)
    rinv = jnp.concatenate([top, bot], axis=0)
    hi = rinv.astype(jnp.bfloat16)
    rest = rinv - hi.astype(jnp.float32)
    mid = rest.astype(jnp.bfloat16)
    lo = (rest - mid.astype(jnp.float32)).astype(jnp.bfloat16)
    def modes(n, carry):
        x = lead_ref[pl.ds(pl.multiple_of(n * 256, 256), 256), :]
        y = jnp.dot(x, lo, preferred_element_type=jnp.float32)
        y = y + jnp.dot(x, mid, preferred_element_type=jnp.float32)
        y = y + jnp.dot(x, hi, preferred_element_type=jnp.float32)
        basis_ref[pl.ds(n * 32, 32), :, :] = y.reshape(32, 8, 256).astype(jnp.bfloat16)
        return carry
    lax.fori_loop(0, 4, modes, 0)

def factor_and_modes(gram_blocks, lead):
    V = pl.BlockSpec(memory_space=pltpu.VMEM)
    return pl.pallas_call(
        k2_body,
        out_shape=(jax.ShapeDtypeStruct((128, 8, 256), jnp.bfloat16), jax.ShapeDtypeStruct((512, 512), jnp.float32)),
        in_specs=[V, V], out_specs=(V, V),
        scratch_shapes=[pltpu.VMEM((512, 512), jnp.float32), pltpu.VMEM((4, 128, 128), jnp.float32)],
        compiler_params=pltpu.CompilerParams(vmem_limit_bytes=32 << 20),
        name="factor_modes",
    )(gram_blocks, lead)


def on_device(operators, excitations, comp_scale, live_count, port_of):
    gram_blocks, lead = gather_and_sum(operators, excitations, comp_scale, live_count, port_of.reshape(1, 128))
    return factor_and_modes(gram_blocks, lead)


def solution(mesh):
    placed = (P("comp", "col", None), P("comp", None, "col"), P("comp"), P("comp"), P("comp", "col"))
    return jax.shard_map(on_device, mesh=mesh, in_specs=placed, out_specs=(P(("comp", "col"), None, None), P()), check_vma=False)
```

time: 581 us -> 147 us (0.25)
  waiting for transfers between devices: 370 us -> 0 us
  Pallas kernels: 0 us -> 140 us
  other arithmetic: 103 us -> 0 us
  starting transfers between devices: 51 us -> 0 us
  between operations: 17.2 us -> 1.29 us
  matrix products: 15 us -> 0 us
  local copies, waits for them, and re-layouts: 16.1 us -> 4.6 us
    psum x1 -> x0, waiting for transfers between devices: 253 us -> none  [on_device(): gram_sum = lax.psum(local_gram, ('comp', 'col'))]
    pallas_call x0 -> x2, Pallas kernels: none -> 140 us  [the longest x1 116 us: gather_and_sum(): pl.pallas_call(gather_kernel, out_shape=(jax.ShapeDtypeStruct((10, 128, 1...]
    another operation x17 -> x0, other arithmetic: 98.5 us -> none  [the longest x14 78.8 us: factorize(): lower = jnp.linalg.cholesky(gram)]
    all_gather x1 -> x0, waiting for transfers between devices: 96.1 us -> none  [on_device(): lax.all_gather(operators, 'col', axis=1, tiled=True)]
    all_to_all x3 -> x0, starting transfers between devices: 51 us -> none  [the longest x1 41 us: on_device(): lax.all_to_all(labels, 'comp', split_axis=0, concat_axis=0, tiled=True)]
    all_to_all x3 -> x0, waiting for transfers between devices: 20.6 us -> none  [the longest x1 11.3 us: on_device(): lax.all_to_all(labels, 'comp', split_axis=0, concat_axis=0, tiled=True)]
    dot_general x6 -> x0, matrix products: 8.68 us -> none  [the longest x2 4.8 us: advance(): jnp.dot(operator_one, excite_one, preferred_element_type=jnp.float32)]
    another operation x9 -> x0, matrix products: 6.3 us -> none  [the longest x6 5.47 us: factorize(): lower = jnp.linalg.cholesky(gram)]
  transfers between devices with their start and end apart: 5 -> 0, of which waited for: 4 -> 0; matrix products, arithmetic and copies ran while one was open for 21% -> 0% of each run, Pallas kernels for 0% -> 0%
where the time goes in v1:
time: 147 us; the launch traced here: 146 us
  Pallas kernels  140 us (95%)
  local copies, waits for them, and re-layouts  4.6 us (3%)
    pallas_call x1, Pallas kernels, gather_and_sum(): pl.pallas_call(gather_kernel, out_shape=(jax.ShapeDtypeStruct((10, 128, 1...  116 us
    pallas_call x1, Pallas kernels, factor_and_modes(): pl.pallas_call(k2_body, out_shape=(jax.ShapeDtypeStruct((128, 8, 256), jn...  24 us
    unnamed x6, local copies, waits for them, and re-layouts  3.84 us

profile of v1, /device:TPU:1, one launch (start us, length us, event | category | flops | bytes accessed | tf_op | source)
XLA Modules:
  0.0 146.0 jit_solution(598201785083535919)
XLA Ops:
  1.3 0.8 reshape.7.ports
  2.0 0.0 copy-start
  2.0 1.6 %copy-done = bf16[8,128,1024]{2,1,0:T(8,128)(2,1)S(1)} copy-done((bf16[8,128,1024]{2,1,0:T(8,128)(2,1)S(1)}, bf16[8,128,1024]{2,1,0:T(8,128)(2,1)}, u32[]{:S(2)}) %copy-start) | copy-done | bytes 2097176
  3.6 0.0 copy-start.1
  3.6 1.6 %copy-done.1 = bf16[8,1024,128]{2,1,0:T(8,128)(2,1)S(1)} copy-done((bf16[8,1024,128]{2,1,0:T(8,128)(2,1)S(1)}, bf16[8,1024,128]{2,1,0:T(8,128)(2,1)}, u32[]{:S(2)}) %copy-start.1) | copy-done | bytes 2097176
  5.2 0.0 copy-start.2
  5.2 0.7 copy-done.2
  5.9 116.1 %gather_and_sum.1 = (f32[10,128,128]{2,1,0:T(8,128)S(1)}, bf16[1024,256]{1,0:T(8,128)(2,1)S(1)}) custom-call(bf16[8,128,1024]{2,1,0:T(8,128)(2,1)S(1)} %copy-done, bf16[8,1024,128]{2,1,0:T(8,128)(2,1)S(1)} %copy-done.1, f32[8]{0:T(128)S(1)} %copy-done.2, s32[1]{0:T(128)S(6)} %copy.7.live, s32[1,128]{1,0:T(1,128)S(1)} %reshape.7.ports), custom_call_target="tpu_custom_call" | custom-call | tf_op jit(solution)/shard_map/gather_and_sum/pallas_call | solution.py:299
  122.0 24.0 %factor_modes.1 = (bf16[128,8,256]{2,1,0:T(8,128)(2,1)}, f32[512,512]{1,0:T(8,128)}) custom-call(f32[10,128,128]{2,1,0:T(8,128)S(1)} %get-tuple-element.4.g_ref, bf16[1024,256]{1,0:T(8,128)(2,1)S(1)} %get-tuple-element.5.lead_ref), custom_call_target="tpu_custom_call" | custom-call | tf_op jit(solution)/shard_map/factor_modes/pallas_call | solution.py:386
Async XLA Ops:
  2.0 1.6 %copy-start = (bf16[8,128,1024]{2,1,0:T(8,128)(2,1)S(1)}, bf16[8,128,1024]{2,1,0:T(8,128)(2,1)}, u32[]{:S(2)}) copy-start(bf16[8,128,1024]{2,1,0:T(8,128)(2,1)} %ops.1) | copy-start | bytes 6291460
  3.6 1.6 %copy-start.1 = (bf16[8,1024,128]{2,1,0:T(8,128)(2,1)S(1)}, bf16[8,1024,128]{2,1,0:T(8,128)(2,1)}, u32[]{:S(2)}) copy-start(bf16[8,1024,128]{2,1,0:T(8,128)(2,1)} %exc.1) | copy-start | bytes 6291460
  5.2 0.7 copy-start.2

commit v2 on v1

v2 whole, which is shorter than its diff:
```python
import jax
import jax.numpy as jnp
from jax import lax
from jax.experimental import pallas as pl
from jax.experimental.pallas import tpu as pltpu
from jax.sharding import PartitionSpec as P

MESH = pl.DeviceIdType.MESH
NX, NY, NZ, NT = 4, 8, 8, 16
F32, BF16, I32 = jnp.float32, jnp.bfloat16, jnp.int32
FIRST = [(0, 0), (0, 1), (0, 2), (0, 3), (1, 1)]
SECOND = [(1, 2), (1, 3), (2, 2), (2, 3), (3, 3)]


CUT_Z, CUT_T = (0, 0, 3, 5, 7), (0, 0, 6, 11, 15)
HI = lax.Precision.HIGHEST


def iota(shape, dim):
    return lax.broadcasted_iota(I32, shape, dim)


def dot_hi(a, b, ta=False):
    dims = (((0,), (0,)), ((), ())) if ta else (((1,), (0,)), ((), ()))
    return lax.dot_general(a, b, dims, precision=HI, preferred_element_type=jnp.float32)

def factor_block(S):
    sub = lax.broadcasted_iota(jnp.int32, (8, 128), 0)
    lane = lax.broadcasted_iota(jnp.int32, (8, 128), 1)
    S = list(S)
    T = [(lane == sub + 8 * i).astype(jnp.float32) for i in range(16)]
    for j in range(16):
        B = {i: [jnp.broadcast_to(S[i][:, 8 * j + k:8 * j + k + 1], (8, 128)) for k in range(8)] for i in range(j, 16)}
        scale = jnp.zeros((8, 128), jnp.float32)
        for k in range(8):
            piv = B[j][k][k:k + 1, :]
            inv = 1.0 / piv
            scale = jnp.where(sub == k, lax.rsqrt(piv), scale)
            prow, qrow = S[j][k:k + 1, :], T[j][k:k + 1, :]
            brow = [B[j][kk][k:k + 1, :] for kk in range(8)]
            for i in range(j, 16):
                m = B[i][k] * inv
                if i == j:
                    m = jnp.where(sub > k, m, 0.0)
                if i > j or k < 7:
                    S[i] = S[i] - m * prow
                    T[i] = T[i] - m * qrow
                    for kk in range(k + 1, 8):
                        B[i][kk] = B[i][kk] - m * brow[kk]
        S[j] = jnp.where(lane >= sub + 8 * j, S[j], 0.0) * scale
        T[j] = T[j] * scale
    return S, T


def factor_rows(S, T, upper, after_first, row_done):
    def step(kb, carry):
        r0 = pl.multiple_of(kb * 128, 128)
        U, inverse = factor_block([S[pl.ds(r0 + 8 * i, 8), pl.ds(r0, 128)] for i in range(16)])
        for i in range(16):
            T[kb, 8 * i:8 * i + 8, :] = inverse[i]
            upper[pl.ds(r0 + 8 * i, 8), pl.ds(r0, 128)] = U[i]
        for n in range(4):
            @pl.when(kb == n)
            def _(n=n):
                edge = (n + 1) * 128
                if n == 0:
                    after_first()
                if n < 3:
                    row = dot_hi(T[n], S[n * 128:edge, edge:])
                    upper[n * 128:edge, edge:] = row
                row_done(n)
                for r in range(n + 1, 4):
                    right = row[:, r * 128 - edge:]
                    S[r * 128:r * 128 + 128, r * 128:] = S[r * 128:r * 128 + 128, r * 128:] - dot_hi(right[:, 0:128], right, ta=True)
        return carry
    lax.fori_loop(0, 4, step, 0)


def finish_kernel(upper_in, pieces_hbm, lead_hbm, basis, upper, passing, pieces, lead, out, sems):
    half = [pl.ds(n * 256, 256) for n in range(4)]
    whole = [pltpu.make_async_copy(upper_in.at[half[n], :], passing.at[half[n], :], sems.at[n]) for n in range(2)]
    copies = [pltpu.make_async_copy(pieces_hbm, pieces, sems.at[2])]
    copies += [pltpu.make_async_copy(lead_hbm.at[half[n], :], lead.at[half[n], :], sems.at[3 + n]) for n in range(4)]
    for copy in copies + whole:
        copy.start()
    back = []
    for n in range(2):
        whole[n].wait()
        back.append(pltpu.make_async_copy(passing.at[half[n], :], upper.at[half[n], :], sems.at[11 + n]))
        back[n].start()
    copies[0].wait()
    for n in range(4):
        copies[1 + n].wait()
        block = lead[half[n], :]
        total = jnp.dot(block, pieces[2], preferred_element_type=F32)
        total = total + jnp.dot(block, pieces[1], preferred_element_type=F32)
        total = total + jnp.dot(block, pieces[0], preferred_element_type=F32)
        out[pl.ds(n * 32, 32)] = total.reshape(32, 8, 256).astype(BF16)
        back.append(pltpu.make_async_copy(out.at[pl.ds(n * 32, 32)], basis.at[pl.ds(n * 32, 32)], sems.at[7 + n]))
        back[2 + n].start()
    for copy in back:
        copy.wait()


def finish(upper, pieces, lead):
    H = pl.BlockSpec(memory_space=pl.ANY)
    return pl.pallas_call(
        finish_kernel,
        out_shape=(jax.ShapeDtypeStruct((128, 8, 256), BF16), jax.ShapeDtypeStruct((512, 512), F32)),
        in_specs=[H] * 3, out_specs=(H, H),
        scratch_shapes=[pltpu.VMEM((512, 512), F32), pltpu.VMEM((3, 256, 256), BF16), pltpu.VMEM((1024, 256), BF16),
                        pltpu.VMEM((128, 8, 256), BF16), pltpu.SemaphoreType.DMA((13,))],
        compiler_params=pltpu.CompilerParams(vmem_limit_bytes=60 << 20),
        name="modes",
    )(upper, pieces, lead)


def fused_kernel(ops, exc, scale_hbm, live_hbm, ports_hbm, upper_hbm, pieces_hbm, lead_hbm,
                 A, E, W, lead, P_pack, P_un, ports, scale, live, pmine, pz, ptile, pall,
                 PA, PB, RA1, RA2, RB1, RB2,
                 S, T, upper, pieces, lead_out, out_sem, g0, g1, r0c, r1c, s0, s1, rz0, ry1, t0, t1, ry0, rz1, u0, u1, rx0, rx1,
                 ay0, az1, az0, ay1, f0, f1,
                 local_sem, s_ops, r_ops, s_exc, r_exc, s_pz, r_pz, s_py, r_py, s_ld, r_ld,
                 s_core, r_core, s_red, r_red, s_x, r_x, s_rel, r_rel):
    comp, x = lax.axis_index("comp"), lax.axis_index("col")
    z, y, core = comp // 16, (comp // 2) % 8, comp % 2
    t = y * 2 + core

    def at(xx=None, yy=None, zz=None, cc=None):
        xx, yy, zz, cc = (x if xx is None else xx, y if yy is None else yy, z if zz is None else zz, core if cc is None else cc)
        return ((zz * 8 + yy) * 2 + cc, xx)

    def at_t(tt):
        return (z * 16 + tt, x)

    started = []

    def send(src, dst, ss, rs, to):
        copy = pltpu.make_async_remote_copy(src_ref=src, dst_ref=dst, send_sem=ss, recv_sem=rs, device_id=to, device_id_type=MESH)
        copy.start()
        started.append(copy)

    def arrived(dst, ss, rs, frm):
        pltpu.make_async_remote_copy(src_ref=dst, dst_ref=dst, send_sem=ss, recv_sem=rs, device_id=frm, device_id_type=MESH).wait_recv()

    xs = [(d, lax.rem(x + d, NX), lax.rem(x + NX - d, NX)) for d in (1, 3, 2)]
    ys = [(d, lax.rem(y + d, NY), lax.rem(y + NY - d, NY)) for d in (4, 3, 5, 2, 6, 1, 7)]
    zs = [(d, lax.rem(z + d, NZ), lax.rem(z + NZ - d, NZ)) for d in (4, 3, 5, 2, 6, 1, 7)]
    ts = [(d, lax.rem(t + d, NT), lax.rem(t + NT - d, NT)) for d in (8, 7, 9, 6, 10, 5, 11, 4, 12, 3, 13, 2, 14, 1, 15)]
    other = 1 - core

    barrier = pltpu.get_barrier_semaphore()
    for _, to, _ in xs:
        pl.semaphore_signal(barrier, inc=1, device_id=at(xx=to), device_id_type=MESH)
    for _, to, _ in zs:
        pl.semaphore_signal(barrier, inc=1, device_id=at(zz=to), device_id_type=MESH)
    for _, to, _ in ts:
        pl.semaphore_signal(barrier, inc=1, device_id=at_t(to), device_id_type=MESH)

    small = [pltpu.make_async_copy(ports_hbm, ports, local_sem.at[4]),
             pltpu.make_async_copy(scale_hbm, scale, local_sem.at[5]),
             pltpu.make_async_copy(live_hbm, live, local_sem.at[6])]
    for copy in small:
        copy.start()
    own = []
    for k in range(2):
        own.append(pltpu.make_async_copy(ops.at[2 * x + k], A.at[k, pl.ds(pl.multiple_of(x * 128, 128), 128), :], local_sem.at[k]))
        own.append(pltpu.make_async_copy(exc.at[2 * x + k], E.at[k, :, pl.ds(pl.multiple_of(x * 128, 128), 128)], local_sem.at[2 + k]))
    for copy in own:
        copy.start()
    pl.semaphore_wait(barrier, 3 + 7 + 15)

    rows_me = pl.ds(pl.multiple_of(x * 128, 128), 128)
    for k in range(2):
        for d, to, _ in xs:
            send(ops.at[2 * to + k], A.at[k, rows_me, :], s_ops.at[k, d - 1], r_ops.at[k, d - 1], at(xx=to))
            send(exc.at[2 * to + k], E.at[k, :, rows_me], s_exc.at[k, d - 1], r_exc.at[k, d - 1], at(xx=to))

    for copy in small:
        copy.wait()
    pick = (iota((16, 128), 1) % 16 == iota((16, 128), 0)).astype(F32).astype(BF16)
    p_high = jnp.dot((ports[...] // 256).astype(F32).astype(BF16), pick, preferred_element_type=F32)
    p_low = jnp.dot((ports[...] % 256).astype(F32).astype(BF16), pick, preferred_element_type=F32)
    p_local = jnp.where(iota((8, 128), 1) // 16 == iota((8, 128), 0), p_high * 256 + p_low, 0.0)
    p_local = jnp.sum(p_local, axis=0, keepdims=True).astype(I32)
    pmine[...] = jnp.broadcast_to(p_local, (8, 128)).astype(F32)
    pz[z] = pmine[...]
    for d, to, _ in zs:
        send(pmine, pz.at[z], s_pz.at[d - 1], r_pz.at[d - 1], at(zz=to))
    target = p_local // 512
    target_all = jnp.broadcast_to(target.astype(F32), (128, 128))
    target_col = target_all.T
    earlier = (target_col == target_all) & (iota((128, 128), 0) < iota((128, 128), 1))
    rank = jnp.sum(earlier.astype(F32), axis=0, keepdims=True)
    base = jnp.broadcast_to(target.astype(F32) * 2 + rank, (8, 128)).astype(BF16)
    spread = (iota((128, 1024), 1) // 8 == iota((128, 1024), 0)).astype(BF16)
    key = jnp.dot(base, spread, preferred_element_type=F32)[0:1, :].astype(I32) * 8 + iota((1, 1024), 1) % 8

    def fill_pack(n, carry):
        P_pack[pl.ds(pl.multiple_of(n * 128, 128), 128), :] = (iota((128, 1024), 0) + n * 128 == key).astype(F32).astype(BF16)
        return carry
    lax.fori_loop(0, 16, fill_pack, 0)

    for d, _, frm in zs:
        arrived(pz.at[frm], s_pz.at[d - 1], r_pz.at[d - 1], at(zz=frm))
    tile = jnp.concatenate([pz[n, 0:1, :] for n in range(8)], axis=0)
    ptile[...] = tile
    pall[t] = tile
    for d, to, _ in ts:
        send(ptile, pall.at[t], s_py.at[d - 1], r_py.at[d - 1], at_t(to))
    for d, _, frm in ts:
        arrived(pall.at[frm], s_py.at[d - 1], r_py.at[d - 1], at_t(frm))
    every = pall[...].reshape(128, 128).astype(I32)
    mine = jnp.where(every // 512 == comp, every % 128 + 1, 0).astype(F32).T
    is_mine = (mine > 0.5)
    below = (iota((128, 128), 1) < iota((128, 128), 0)).astype(BF16)
    order = jnp.dot(below, is_mine.astype(F32).astype(BF16), preferred_element_type=F32)
    zero = jnp.zeros((128, 128), F32)
    first = jnp.sum(jnp.where(is_mine & (order < 0.5), mine, zero), axis=0, keepdims=True)
    second = jnp.sum(jnp.where(is_mine & (order > 0.5), mine, zero), axis=0, keepdims=True)
    both = jnp.concatenate([first, second, jnp.zeros((6, 128), F32)], axis=0).astype(BF16)
    lane = iota((128, 2048), 1) // 16
    widen = ((lane % 16) * 8 + lane // 16 == iota((128, 2048), 0)).astype(F32).astype(BF16)
    wide = jnp.dot(both, widen, preferred_element_type=F32)
    which = (iota((1, 2048), 1) // 8) % 2
    place = jnp.where(which == 0, wide[0:1, :], wide[1:2, :]).astype(I32) * 8 - 8 + iota((1, 2048), 1) % 8

    def fill_un(n, carry):
        P_un[pl.ds(pl.multiple_of(n * 128, 128), 128), :] = (iota((128, 2048), 0) + n * 128 == place).astype(F32).astype(BF16)
        return carry
    lax.fori_loop(0, 8, fill_un, 0)

    def send_leads(k):
        for d, to, _ in xs:
            send(W.at[k, pl.ds(pl.multiple_of(to * 128, 128), 128), pl.ds(0, 256)], lead.at[2 * x + k], s_ld.at[k, d - 1], r_ld.at[k, d - 1], at(xx=to))
        lead[2 * x + k] = W[k, rows_me, 0:256]

    for copy in own:
        copy.wait()
    for k in range(2):
        for d, _, frm in xs:
            there = pl.ds(pl.multiple_of(frm * 128, 128), 128)
            arrived(A.at[k, there, :], s_ops.at[k, d - 1], r_ops.at[k, d - 1], at(xx=frm))
            arrived(E.at[k, :, there], s_exc.at[k, d - 1], r_exc.at[k, d - 1], at(xx=frm))
        slot = 2 * x + k
        alive = jnp.minimum(jnp.maximum(live[0] - slot, 0), 1).astype(F32)
        weight = scale[slot] * alive

        def rows(n, carry):
            where = pl.ds(pl.multiple_of(n * 256, 256), 256)
            product = jnp.dot(A[k, where, :], E[k], preferred_element_type=F32)
            W[k, where, :] = (product * weight).astype(BF16)
            return carry
        lax.fori_loop(0, 2, rows, 0)
        if k == 0:
            send_leads(0)
        for r in range(4):
            out = lax.dot_general(W[k, :, r * 128:(r + 1) * 128], W[k, :, r * 128:], (((0,), (0,)), ((), ())), preferred_element_type=F32)
            for c in range(r, 4):
                g, n = (g0, FIRST.index((r, c))) if (r, c) in FIRST else (g1, SECOND.index((r, c)))
                part = out[:, (c - r) * 128:(c - r + 1) * 128]
                g[n * 128:(n + 1) * 128, :] = part if k == 0 else g[n * 128:(n + 1) * 128, :] + part
            if k == 1 and r == 1:
                send(g0.at[pl.ds(pl.multiple_of(other * 320, 64), 320), :], r0c, s_core.at[0], r_core.at[0], at(cc=other))
    send(g1.at[pl.ds(pl.multiple_of(other * 320, 64), 320), :], r1c, s_core.at[1], r_core.at[1], at(cc=other))
    send_leads(1)
    arrived(r0c, s_core.at[0], r_core.at[0], at(cc=other))
    s0[...] = g0[pl.ds(pl.multiple_of(core * 320, 64), 320), :] + r0c[...]
    for d, to, _ in zs:
        send(s0.at[pl.ds(pl.multiple_of(to * 40, 8), 40), :], rz0.at[z], s_red.at[0, d - 1], r_red.at[0, d - 1], at(zz=to))
    arrived(r1c, s_core.at[1], r_core.at[1], at(cc=other))
    s1[...] = g1[pl.ds(pl.multiple_of(core * 320, 64), 320), :] + r1c[...]
    for d, to, _ in ys:
        send(s1.at[pl.ds(pl.multiple_of(to * 40, 8), 40), :], ry1.at[y], s_red.at[1, d - 1], r_red.at[1, d - 1], at(yy=to))
    rz0[z] = s0[pl.ds(pl.multiple_of(z * 40, 8), 40), :]
    ry1[y] = s1[pl.ds(pl.multiple_of(y * 40, 8), 40), :]

    for k in range(2):
        for d, _, frm in xs:
            arrived(lead.at[2 * frm + k], s_ld.at[k, d - 1], r_ld.at[k, d - 1], at(xx=frm))

    def pack(n, carry):
        packed = jnp.dot(P_pack[pl.ds(pl.multiple_of(n * 256, 256), 256), :], lead[...].reshape(1024, 256), preferred_element_type=F32).astype(BF16)
        PA[pl.ds(n * 16, 16)] = packed[:, 0:128].reshape(16, 16, 128)
        PB[n] = packed[:, 128:256].reshape(16, 16, 128)
        return carry
    lax.fori_loop(0, 8, pack, 0)

    def first_leg(bunch):
        for d, to, _ in zs[CUT_Z[bunch]:CUT_Z[bunch + 1]]:
            send(PA.at[pl.ds(to * 16, 16)], RA1.at[z], s_rel.at[0, d - 1], r_rel.at[0, d - 1], at(zz=to))
        for d, to, _ in ts[CUT_T[bunch]:CUT_T[bunch + 1]]:
            send(PB.at[:, to], RB1.at[t], s_rel.at[1, d - 1], r_rel.at[1, d - 1], at_t(to))

    def second_leg():
        for d, _, frm in zs:
            arrived(RA1.at[frm], s_rel.at[0, d - 1], r_rel.at[0, d - 1], at(zz=frm))
        for d, to, _ in ts:
            send(RA1.at[:, to], RA2.at[:, t], s_rel.at[2, d - 1], r_rel.at[2, d - 1], at_t(to))
        RA2[:, t] = RA1[:, t]
        for d, _, frm in ts:
            arrived(RB1.at[frm], s_rel.at[1, d - 1], r_rel.at[1, d - 1], at_t(frm))
        for d, to, _ in zs:
            send(RB1.at[:, to], RB2.at[z], s_rel.at[3, d - 1], r_rel.at[3, d - 1], at(zz=to))
        RB2[z] = RB1[:, z]

    first_leg(0)
    RA1[z] = PA[pl.ds(z * 16, 16)]
    RB1[t] = PB[:, t]
    for d, _, frm in zs:
        arrived(rz0.at[frm], s_red.at[0, d - 1], r_red.at[0, d - 1], at(zz=frm))
    t0[0:40, :] = sum([rz0[n] for n in range(1, 8)], rz0[0])
    t0[40:64, :] = jnp.zeros((24, 128), F32)
    for d, to, _ in ys:
        send(t0.at[pl.ds(pl.multiple_of(to * 8, 8), 8), :], ry0.at[y], s_red.at[2, d - 1], r_red.at[2, d - 1], at(yy=to))
    ry0[y] = t0[pl.ds(pl.multiple_of(y * 8, 8), 8), :]
    for d, _, frm in ys:
        arrived(ry1.at[frm], s_red.at[1, d - 1], r_red.at[1, d - 1], at(yy=frm))
    t1[0:40, :] = sum([ry1[n] for n in range(1, 8)], ry1[0])
    t1[40:64, :] = jnp.zeros((24, 128), F32)
    for d, to, _ in zs:
        send(t1.at[pl.ds(pl.multiple_of(to * 8, 8), 8), :], rz1.at[z], s_red.at[3, d - 1], r_red.at[3, d - 1], at(zz=to))
    rz1[z] = t1[pl.ds(pl.multiple_of(z * 8, 8), 8), :]

    first_leg(1)
    for d, _, frm in ys:
        arrived(ry0.at[frm], s_red.at[2, d - 1], r_red.at[2, d - 1], at(yy=frm))
    u0[...] = sum([ry0[n] for n in range(1, 8)], ry0[0])
    for d, to, _ in xs:
        send(u0, rx0.at[x], s_x.at[0, d - 1], r_x.at[0, d - 1], at(xx=to))
    rx0[x] = u0[...]
    for d, _, frm in zs:
        arrived(rz1.at[frm], s_red.at[3, d - 1], r_red.at[3, d - 1], at(zz=frm))
    u1[...] = sum([rz1[n] for n in range(1, 8)], rz1[0])
    for d, to, _ in xs:
        send(u1, rx1.at[x], s_x.at[1, d - 1], r_x.at[1, d - 1], at(xx=to))
    rx1[x] = u1[...]
    first_leg(2)

    for d, _, frm in xs:
        arrived(rx0.at[frm], s_x.at[0, d - 1], r_x.at[0, d - 1], at(xx=frm))
    ay0[pl.ds(pl.multiple_of(y * 8, 8), 8), :] = (rx0[0] + rx0[1]) + (rx0[2] + rx0[3])
    mine0 = ay0.at[pl.ds(pl.multiple_of(y * 8, 8), 8), :]
    for d, to, _ in ys:
        send(mine0, mine0, s_red.at[4, d - 1], r_red.at[4, d - 1], at(yy=to))
    for d, _, frm in xs:
        arrived(rx1.at[frm], s_x.at[1, d - 1], r_x.at[1, d - 1], at(xx=frm))
    az1[pl.ds(pl.multiple_of(z * 8, 8), 8), :] = (rx1[0] + rx1[1]) + (rx1[2] + rx1[3])
    mine1 = az1.at[pl.ds(pl.multiple_of(z * 8, 8), 8), :]
    for d, to, _ in zs:
        send(mine1, mine1, s_red.at[5, d - 1], r_red.at[5, d - 1], at(zz=to))

    first_leg(3)
    for d, _, frm in ys:
        arrived(ay0.at[pl.ds(pl.multiple_of(frm * 8, 8), 8), :], s_red.at[4, d - 1], r_red.at[4, d - 1], at(yy=frm))
    az0[z] = ay0[0:40, :]
    for d, to, _ in zs:
        send(ay0.at[0:40, :], az0.at[z], s_red.at[6, d - 1], r_red.at[6, d - 1], at(zz=to))
    for d, _, frm in zs:
        arrived(az1.at[pl.ds(pl.multiple_of(frm * 8, 8), 8), :], s_red.at[5, d - 1], r_red.at[5, d - 1], at(zz=frm))
    ay1[y] = az1[0:40, :]
    for d, to, _ in ys:
        send(az1.at[0:40, :], ay1.at[y], s_red.at[7, d - 1], r_red.at[7, d - 1], at(yy=to))

    for d, _, frm in zs:
        arrived(az0.at[frm], s_red.at[6, d - 1], r_red.at[6, d - 1], at(zz=frm))
    f0[core] = az0[...].reshape(320, 128)
    mine_f0 = f0.at[core]
    send(mine_f0, mine_f0, s_core.at[2], r_core.at[2], at(cc=other))
    for d, _, frm in ys:
        arrived(ay1.at[frm], s_red.at[7, d - 1], r_red.at[7, d - 1], at(yy=frm))
    f1[core] = ay1[...].reshape(320, 128)
    mine_f1 = f1.at[core]
    send(mine_f1, mine_f1, s_core.at[3], r_core.at[3], at(cc=other))

    second_leg()
    arrived(f0.at[other], s_core.at[2], r_core.at[2], at(cc=other))

    def fill(f, blocks):
        for n, (r, c) in enumerate(blocks):
            for part in range(n * 128, n * 128 + 128, 64):
                row = r * 128 + part - n * 128
                S[row:row + 64, c * 128:(c + 1) * 128] = f[part // 320, part % 320:part % 320 + 64, :] * (1.0 / 524288)

    def after_first():
        arrived(f1.at[other], s_core.at[3], r_core.at[3], at(cc=other))
        fill(f1, SECOND)

    def row_copy(n):
        rows = pl.ds(n * 128, 128)
        return pltpu.make_async_copy(upper.at[rows, :], upper_hbm.at[rows, :], out_sem.at[n])

    for r in range(1, 4):
        upper[r * 128:(r + 1) * 128, 0:r * 128] = jnp.zeros((128, r * 128), F32)
    fill(f0, FIRST)
    factor_rows(S, T, upper, after_first, lambda n: row_copy(n).start())
    t0, t1 = T[0].T, T[1].T
    cross = -dot_hi(t0, dot_hi(upper[0:128, 128:256], t1))
    bottom = jnp.concatenate([jnp.zeros((128, 128), F32), t1], axis=1)
    inverse = jnp.concatenate([jnp.concatenate([t0, cross], axis=1), bottom], axis=0)
    pieces[0] = inverse.astype(BF16)
    left = inverse - pieces[0].astype(F32)
    pieces[1] = left.astype(BF16)
    pieces[2] = (left - pieces[1].astype(F32)).astype(BF16)
    pieces_copy = pltpu.make_async_copy(pieces, pieces_hbm, out_sem.at[4])
    pieces_copy.start()
    for d, _, frm in ts:
        arrived(RA2.at[:, frm], s_rel.at[2, d - 1], r_rel.at[2, d - 1], at_t(frm))
    for d, _, frm in zs:
        arrived(RB2.at[frm], s_rel.at[3, d - 1], r_rel.at[3, d - 1], at(zz=frm))

    lead_copies = []
    for n in range(4):
        where = pl.ds(n * 256, 256)
        choose = P_un[where, :]
        lead_out[where, 0:128] = jnp.dot(choose, RA2[...].reshape(2048, 128), preferred_element_type=F32).astype(BF16)
        lead_out[where, 128:256] = jnp.dot(choose, RB2[...].reshape(2048, 128), preferred_element_type=F32).astype(BF16)
        lead_copies.append(pltpu.make_async_copy(lead_out.at[where, :], lead_hbm.at[where, :], out_sem.at[5 + n]))
        lead_copies[n].start()
    for copy in started:
        copy.wait_send()
    for copy in [row_copy(n) for n in range(4)] + [pieces_copy] + lead_copies:
        copy.wait()


def fused(ops, exc, scale, live, ports):
    D = pltpu.SemaphoreType.DMA
    vm = pltpu.VMEM
    H = pl.BlockSpec(memory_space=pl.ANY)
    scratch = [
        vm((2, 512, 1024), BF16), vm((2, 1024, 512), BF16), vm((2, 512, 512), BF16), vm((8, 128, 256), BF16),
        vm((2048, 1024), BF16), vm((1024, 2048), BF16),
        vm((8, 16), I32), pltpu.SMEM((8,), F32), pltpu.SMEM((1,), I32),
        vm((8, 128), F32), vm((8, 8, 128), F32), vm((8, 128), F32), vm((16, 8, 128), F32),
        vm((128, 16, 128), BF16), vm((8, 16, 16, 128), BF16),
        vm((8, 16, 16, 128), BF16), vm((8, 16, 16, 128), BF16), vm((16, 8, 16, 128), BF16), vm((8, 16, 16, 128), BF16),
        vm((512, 512), F32), vm((4, 128, 128), F32), vm((512, 512), F32), vm((3, 256, 256), BF16), vm((1024, 256), BF16), D((9,)),
        vm((640, 128), F32), vm((640, 128), F32), vm((320, 128), F32), vm((320, 128), F32),
        vm((320, 128), F32), vm((320, 128), F32),
        vm((8, 40, 128), F32), vm((8, 40, 128), F32), vm((64, 128), F32), vm((64, 128), F32),
        vm((8, 8, 128), F32), vm((8, 8, 128), F32), vm((8, 128), F32), vm((8, 128), F32),
        vm((4, 8, 128), F32), vm((4, 8, 128), F32),
        vm((64, 128), F32), vm((64, 128), F32), vm((8, 40, 128), F32), vm((8, 40, 128), F32),
        vm((2, 320, 128), F32), vm((2, 320, 128), F32),
        D((7,)), D((2, 3)), D((2, 3)), D((2, 3)), D((2, 3)), D((7,)), D((7,)), D((15,)), D((15,)), D((2, 3)), D((2, 3)),
        D((4,)), D((4,)), D((8, 7)), D((8, 7)), D((2, 3)), D((2, 3)), D((4, 15)), D((4, 15)),
    ]
    out = pl.pallas_call(
        fused_kernel,
        out_shape=tuple(jax.ShapeDtypeStruct(*o) for o in (((512, 512), F32), ((3, 256, 256), BF16), ((1024, 256), BF16))),
        in_specs=[H] * 5, out_specs=(H,) * 3,
        scratch_shapes=scratch,
        compiler_params=pltpu.CompilerParams(collective_id=0, has_side_effects=True, vmem_limit_bytes=62 << 20),
        name="fused",
    )(ops, exc, scale, live, ports)
    return finish(*out)


def solution(mesh):
    placed = (P("comp", "col", None), P("comp", None, "col"), P("comp"), P("comp"), P("comp", "col"))
    return jax.shard_map(fused, mesh=mesh, in_specs=placed, out_specs=(P(("comp", "col"), None, None), P()), check_vma=False)
```

time: 147 us -> 124 us (0.84)
  Pallas kernels: 140 us -> 123 us
  local copies, waits for them, and re-layouts: 4.6 us -> 0 us
    pallas_call x2, Pallas kernels: 140 us -> 123 us  [the longest x1 119 us: fused(): pl.pallas_call(fused_kernel, out_shape=tuple((jax.ShapeDtypeStruct(*o) fo...]
    unnamed x6 -> x0, local copies, waits for them, and re-layouts: 3.84 us -> none
where the time goes in v2:
time: 124 us
  Pallas kernels  123 us (99%)
  between operations  1.28 us (1%)
    pallas_call x1, Pallas kernels, fused(): pl.pallas_call(fused_kernel, out_shape=tuple((jax.ShapeDtypeStruct(*o) fo...  119 us
    pallas_call x1, Pallas kernels, finish(): pl.pallas_call(finish_kernel, out_shape=(jax.ShapeDtypeStruct((128, 8, 25...  3.69 us

profile of v2, /device:TPU:1, one launch (start us, length us, event | category | flops | bytes accessed | tf_op | source)
XLA Modules:
  0.0 124.3 jit_solution(14955159635988535192)
XLA Ops:
  1.3 119.3 %fused.1 = (f32[512,512]{1,0:T(8,128)}, bf16[3,256,256]{2,1,0:T(8,128)(2,1)}, bf16[1024,256]{1,0:T(8,128)(2,1)}) custom-call(bf16[8,128,1024]{2,1,0:T(8,128)(2,1)} %ops.1, bf16[8,1024,128]{2,1,0:T(8,128)(2,1)} %exc.1, f32[8]{0:T(128)} %scale_hbm.1, s32[1]{0:T(128)S(6)} %copy.7.live_hbm, s32[8,16]{1,0:T(8,128)} %ports_hbm.1), custom_call_target="tpu_custom_call" | custom-call | tf_op jit(solution)/shard_map/fused/pallas_call | solution.py:448
  120.6 3.7 %modes.1 = (bf16[128,8,256]{2,1,0:T(8,128)(2,1)}, f32[512,512]{1,0:T(8,128)}) custom-call(f32[512,512]{1,0:T(8,128)} %get-tuple-element.5.upper_in, bf16[3,256,256]{2,1,0:T(8,128)(2,1)} %get-tuple-element.6.pieces_hbm, bf16[1024,256]{1,0:T(8,128)(2,1)} %get-tuple-element.7.lead_hbm), custom_call_target="tpu_custom_call" | custom-call | tf_op jit(solution)/shard_map/modes/pallas_call | solution.py:107

commit v3 on v2

--- a/solution.py
+++ b/solution.py
@@ -12,7 +12,7 @@
 SECOND = [(1, 2), (1, 3), (2, 2), (2, 3), (3, 3)]
 
 
-CUT_Z, CUT_T = (0, 0, 3, 5, 7), (0, 0, 6, 11, 15)
+CUT_Z, CUT_T = (0, 0, 2, 4, 7), (0, 0, 4, 8, 15)
 HI = lax.Precision.HIGHEST
 
 
@@ -24,7 +24,7 @@
     dims = (((0,), (0,)), ((), ())) if ta else (((1,), (0,)), ((), ()))
     return lax.dot_general(a, b, dims, precision=HI, preferred_element_type=jnp.float32)
 
-def factor_block(S):
+def factor_block(S, with_inverse=True):
     sub = lax.broadcasted_iota(jnp.int32, (8, 128), 0)
     lane = lax.broadcasted_iota(jnp.int32, (8, 128), 1)
     S = list(S)
@@ -44,7 +44,8 @@
                     m = jnp.where(sub > k, m, 0.0)
                 if i > j or k < 7:
                     S[i] = S[i] - m * prow
-                    T[i] = T[i] - m * qrow
+                    if with_inverse:
+                        T[i] = T[i] - m * qrow
                     for kk in range(k + 1, 8):
                         B[i][kk] = B[i][kk] - m * brow[kk]
         S[j] = jnp.where(lane >= sub + 8 * j, S[j], 0.0) * scale
@@ -59,66 +60,52 @@
         for i in range(16):
             T[kb, 8 * i:8 * i + 8, :] = inverse[i]
             upper[pl.ds(r0 + 8 * i, 8), pl.ds(r0, 128)] = U[i]
-        for n in range(4):
+        for n in range(3):
             @pl.when(kb == n)
             def _(n=n):
                 edge = (n + 1) * 128
                 if n == 0:
                     after_first()
-                if n < 3:
-                    row = dot_hi(T[n], S[n * 128:edge, edge:])
-                    upper[n * 128:edge, edge:] = row
+                row = dot_hi(T[n], S[n * 128:edge, edge:])
+                upper[n * 128:edge, edge:] = row
                 row_done(n)
                 for r in range(n + 1, 4):
                     right = row[:, r * 128 - edge:]
                     S[r * 128:r * 128 + 128, r * 128:] = S[r * 128:r * 128 + 128, r * 128:] - dot_hi(right[:, 0:128], right, ta=True)
         return carry
-    lax.fori_loop(0, 4, step, 0)
-
-
-def finish_kernel(upper_in, pieces_hbm, lead_hbm, basis, upper, passing, pieces, lead, out, sems):
-    half = [pl.ds(n * 256, 256) for n in range(4)]
-    whole = [pltpu.make_async_copy(upper_in.at[half[n], :], passing.at[half[n], :], sems.at[n]) for n in range(2)]
-    copies = [pltpu.make_async_copy(pieces_hbm, pieces, sems.at[2])]
-    copies += [pltpu.make_async_copy(lead_hbm.at[half[n], :], lead.at[half[n], :], sems.at[3 + n]) for n in range(4)]
-    for copy in copies + whole:
+    lax.fori_loop(0, 3, step, 0)
+
+
+def hand_over_kernel(basis_in, upper_in, basis_out, upper_out, basis, upper, sems):
+    parts = [(array.at[pl.ds(n * size, size)], middle.at[pl.ds(n * size, size)], out.at[pl.ds(n * size, size)])
+             for n in range(4) for array, middle, out, size in ((upper_in, upper, upper_out, 128), (basis_in, basis, basis_out, 32))]
+    into = [pltpu.make_async_copy(src, mid, sems.at[0, n]) for n, (src, mid, _) in enumerate(parts)]
+    out = [pltpu.make_async_copy(mid, dst, sems.at[1, n]) for n, (_, mid, dst) in enumerate(parts)]
+    for copy in into:
         copy.start()
-    back = []
-    for n in range(2):
-        whole[n].wait()
-        back.append(pltpu.make_async_copy(passing.at[half[n], :], upper.at[half[n], :], sems.at[11 + n]))
-        back[n].start()
-    copies[0].wait()
-    for n in range(4):
-        copies[1 + n].wait()
-        block = lead[half[n], :]
-        total = jnp.dot(block, pieces[2], preferred_element_type=F32)
-        total = total + jnp.dot(block, pieces[1], preferred_element_type=F32)
-        total = total + jnp.dot(block, pieces[0], preferred_element_type=F32)
-        out[pl.ds(n * 32, 32)] = total.reshape(32, 8, 256).astype(BF16)
-        back.append(pltpu.make_async_copy(out.at[pl.ds(n * 32, 32)], basis.at[pl.ds(n * 32, 32)], sems.at[7 + n]))
-        back[2 + n].start()
-    for copy in back:
+    for first, second in zip(into, out):
+        first.wait()
+        second.start()
+    for copy in out:
         copy.wait()
 
 
-def finish(upper, pieces, lead):
+def hand_over(basis, upper):
     H = pl.BlockSpec(memory_space=pl.ANY)
     return pl.pallas_call(
-        finish_kernel,
+        hand_over_kernel,
         out_shape=(jax.ShapeDtypeStruct((128, 8, 256), BF16), jax.ShapeDtypeStruct((512, 512), F32)),
-        in_specs=[H] * 3, out_specs=(H, H),
-        scratch_shapes=[pltpu.VMEM((512, 512), F32), pltpu.VMEM((3, 256, 256), BF16), pltpu.VMEM((1024, 256), BF16),
-                        pltpu.VMEM((128, 8, 256), BF16), pltpu.SemaphoreType.DMA((13,))],
+        in_specs=[H] * 2, out_specs=(H, H),
+        scratch_shapes=[pltpu.VMEM((128, 8, 256), BF16), pltpu.VMEM((512, 512), F32), pltpu.SemaphoreType.DMA((2, 8))],
         compiler_params=pltpu.CompilerParams(vmem_limit_bytes=60 << 20),
-        name="modes",
-    )(upper, pieces, lead)
-
-
-def fused_kernel(ops, exc, scale_hbm, live_hbm, ports_hbm, upper_hbm, pieces_hbm, lead_hbm,
+        name="hand_over",
+    )(basis, upper)
+
+
+def fused_kernel(ops, exc, scale_hbm, live_hbm, ports_hbm, basis_hbm, upper_hbm,
                  A, E, W, lead, P_pack, P_un, ports, scale, live, pmine, pz, ptile, pall,
                  PA, PB, RA1, RA2, RB1, RB2,
-                 S, T, upper, pieces, lead_out, out_sem, g0, g1, r0c, r1c, s0, s1, rz0, ry1, t0, t1, ry0, rz1, u0, u1, rx0, rx1,
+                 S, T, upper, basis, out_sem, g0, g1, r0c, r1c, s0, s1, rz0, ry1, t0, t1, ry0, rz1, u0, u1, rx0, rx1,
                  ay0, az1, az0, ay1, f0, f1,
                  local_sem, s_ops, r_ops, s_exc, r_exc, s_pz, r_pz, s_py, r_py, s_ld, r_ld,
                  s_core, r_core, s_red, r_red, s_x, r_x, s_rel, r_rel):
@@ -394,32 +381,40 @@
         upper[r * 128:(r + 1) * 128, 0:r * 128] = jnp.zeros((128, r * 128), F32)
     fill(f0, FIRST)
     factor_rows(S, T, upper, after_first, lambda n: row_copy(n).start())
+    for d, _, frm in ts:
+        arrived(RA2.at[:, frm], s_rel.at[2, d - 1], r_rel.at[2, d - 1], at_t(frm))
+    for d, _, frm in zs:
+        arrived(RB2.at[frm], s_rel.at[3, d - 1], r_rel.at[3, d - 1], at(zz=frm))
+
     t0, t1 = T[0].T, T[1].T
     cross = -dot_hi(t0, dot_hi(upper[0:128, 128:256], t1))
     bottom = jnp.concatenate([jnp.zeros((128, 128), F32), t1], axis=1)
     inverse = jnp.concatenate([jnp.concatenate([t0, cross], axis=1), bottom], axis=0)
-    pieces[0] = inverse.astype(BF16)
-    left = inverse - pieces[0].astype(F32)
-    pieces[1] = left.astype(BF16)
-    pieces[2] = (left - pieces[1].astype(F32)).astype(BF16)
-    pieces_copy = pltpu.make_async_copy(pieces, pieces_hbm, out_sem.at[4])
-    pieces_copy.start()
-    for d, _, frm in ts:
-        arrived(RA2.at[:, frm], s_rel.at[2, d - 1], r_rel.at[2, d - 1], at_t(frm))
-    for d, _, frm in zs:
-        arrived(RB2.at[frm], s_rel.at[3, d - 1], r_rel.at[3, d - 1], at(zz=frm))
-
-    lead_copies = []
+    high = inverse.astype(BF16)
+    left = inverse - high.astype(F32)
+    middle = left.astype(BF16)
+    low = (left - middle.astype(F32)).astype(BF16)
+
+    def modes(n):
+        choose = P_un[n * 256:n * 256 + 256, :]
+        one = jnp.dot(choose, RA2[...].reshape(2048, 128), preferred_element_type=F32).astype(BF16)
+        two = jnp.dot(choose, RB2[...].reshape(2048, 128), preferred_element_type=F32).astype(BF16)
+        block = jnp.concatenate([one, two], axis=1)
+        total = jnp.dot(block, low, preferred_element_type=F32)
+        total = total + jnp.dot(block, middle, preferred_element_type=F32)
+        total = total + jnp.dot(block, high, preferred_element_type=F32)
+        basis[n * 32:n * 32 + 32] = total.reshape(32, 8, 256).astype(BF16)
+    last, _ = factor_block([S[384 + 8 * i:392 + 8 * i, 384:512] for i in range(16)], False)
     for n in range(4):
-        where = pl.ds(n * 256, 256)
-        choose = P_un[where, :]
-        lead_out[where, 0:128] = jnp.dot(choose, RA2[...].reshape(2048, 128), preferred_element_type=F32).astype(BF16)
-        lead_out[where, 128:256] = jnp.dot(choose, RB2[...].reshape(2048, 128), preferred_element_type=F32).astype(BF16)
-        lead_copies.append(pltpu.make_async_copy(lead_out.at[where, :], lead_hbm.at[where, :], out_sem.at[5 + n]))
-        lead_copies[n].start()
+        modes(n)
+    for i in range(16):
+        upper[384 + 8 * i:392 + 8 * i, 384:512] = last[i]
+    row_copy(3).start()
+    basis_copy = pltpu.make_async_copy(basis, basis_hbm, out_sem.at[4])
+    basis_copy.start()
     for copy in started:
         copy.wait_send()
-    for copy in [row_copy(n) for n in range(4)] + [pieces_copy] + lead_copies:
+    for copy in [row_copy(n) for n in range(4)] + [basis_copy]:
         copy.wait()
 
 
@@ -434,7 +429,7 @@
         vm((8, 128), F32), vm((8, 8, 128), F32), vm((8, 128), F32), vm((16, 8, 128), F32),
         vm((128, 16, 128), BF16), vm((8, 16, 16, 128), BF16),
         vm((8, 16, 16, 128), BF16), vm((8, 16, 16, 128), BF16), vm((16, 8, 16, 128), BF16), vm((8, 16, 16, 128), BF16),
-        vm((512, 512), F32), vm((4, 128, 128), F32), vm((512, 512), F32), vm((3, 256, 256), BF16), vm((1024, 256), BF16), D((9,)),
+        vm((512, 512), F32), vm((4, 128, 128), F32), vm((512, 512), F32), vm((128, 8, 256), BF16), D((5,)),
         vm((640, 128), F32), vm((640, 128), F32), vm((320, 128), F32), vm((320, 128), F32),
         vm((320, 128), F32), vm((320, 128), F32),
         vm((8, 40, 128), F32), vm((8, 40, 128), F32), vm((64, 128), F32), vm((64, 128), F32),
@@ -447,13 +442,13 @@
     ]
     out = pl.pallas_call(
         fused_kernel,
-        out_shape=tuple(jax.ShapeDtypeStruct(*o) for o in (((512, 512), F32), ((3, 256, 256), BF16), ((1024, 256), BF16))),
-        in_specs=[H] * 5, out_specs=(H,) * 3,
+        out_shape=tuple(jax.ShapeDtypeStruct(*o) for o in (((128, 8, 256), BF16), ((512, 512), F32))),
+        in_specs=[H] * 5, out_specs=(H,) * 2,
         scratch_shapes=scratch,
         compiler_params=pltpu.CompilerParams(collective_id=0, has_side_effects=True, vmem_limit_bytes=62 << 20),
         name="fused",
     )(ops, exc, scale, live, ports)
-    return finish(*out)
+    return hand_over(*out)
 
 
 def solution(mesh):

time: 124 us -> 120 us (0.968)
  Pallas kernels: 123 us -> 118 us
    pallas_call x1, Pallas kernels: 119 us -> 116 us  [fused(): pl.pallas_call(fused_kernel, out_shape=tuple((jax.ShapeDtypeStruct(*o) fo...]
    pallas_call x1, Pallas kernels: 3.69 us -> 2.23 us  [hand_over(): pl.pallas_call(hand_over_kernel, out_shape=(jax.ShapeDtypeStruct((128, 8,...]
where the time goes in v3:
time: 120 us
  Pallas kernels  118 us (98%)
  between operations  1.45 us (1%)
    pallas_call x1, Pallas kernels, fused(): pl.pallas_call(fused_kernel, out_shape=tuple((jax.ShapeDtypeStruct(*o) fo...  116 us

profile of v3, /device:TPU:1, one launch (start us, length us, event | category | flops | bytes accessed | tf_op | source)
XLA Modules:
  0.0 119.7 jit_solution(15118298607899587589)
XLA Ops:
  1.3 116.0 %fused.1 = (bf16[128,8,256]{2,1,0:T(8,128)(2,1)}, f32[512,512]{1,0:T(8,128)}) custom-call(bf16[8,128,1024]{2,1,0:T(8,128)(2,1)} %ops.1, bf16[8,1024,128]{2,1,0:T(8,128)(2,1)} %exc.1, f32[8]{0:T(128)} %scale_hbm.1, s32[1]{0:T(128)S(6)} %copy.7.live_hbm, s32[8,16]{1,0:T(8,128)} %ports_hbm.1), custom_call_target="tpu_custom_call" | custom-call | tf_op jit(solution)/shard_map/fused/pallas_call | solution.py:443
  117.3 2.2 %hand_over.1 = (bf16[128,8,256]{2,1,0:T(8,128)(2,1)}, f32[512,512]{1,0:T(8,128)}) custom-call(bf16[128,8,256]{2,1,0:T(8,128)(2,1)} %get-tuple-element.4.basis_in, f32[512,512]{1,0:T(8,128)} %get-tuple-element.5.upper_in), custom_call_target="tpu_custom_call" | custom-call | tf_op jit(solution)/shard_map/hand_over/pallas_call | solution.py:95

commit v4 on v3

--- a/solution.py
+++ b/solution.py
@@ -30,7 +30,8 @@
     S = list(S)
     T = [(lane == sub + 8 * i).astype(jnp.float32) for i in range(16)]
     for j in range(16):
-        B = {i: [jnp.broadcast_to(S[i][:, 8 * j + k:8 * j + k + 1], (8, 128)) for k in range(8)] for i in range(j, 16)}
+        rows = range(j, 8 if j < 8 else 16)
+        B = {i: [jnp.broadcast_to(S[i][:, 8 * j + k:8 * j + k + 1], (8, 128)) for k in range(8)] for i in rows}
         scale = jnp.zeros((8, 128), jnp.float32)
         for k in range(8):
             piv = B[j][k][k:k + 1, :]
@@ -38,7 +39,7 @@
             scale = jnp.where(sub == k, lax.rsqrt(piv), scale)
             prow, qrow = S[j][k:k + 1, :], T[j][k:k + 1, :]
             brow = [B[j][kk][k:k + 1, :] for kk in range(8)]
-            for i in range(j, 16):
+            for i in rows:
                 m = B[i][k] * inv
                 if i == j:
                     m = jnp.where(sub > k, m, 0.0)
@@ -50,6 +51,13 @@
                         B[i][kk] = B[i][kk] - m * brow[kk]
         S[j] = jnp.where(lane >= sub + 8 * j, S[j], 0.0) * scale
         T[j] = T[j] * scale
+        if j == 7:
+            top = jnp.concatenate(S[0:8], axis=0)
+            change = dot_hi(top, jnp.concatenate([top, jnp.concatenate(T[0:8], axis=0)], axis=1) if with_inverse else top, ta=True)
+            for i in range(8, 16):
+                S[i] = S[i] - change[8 * i:8 * i + 8, 0:128]
+                if with_inverse:
+                    T[i] = T[i] - change[8 * i:8 * i + 8, 128:256]
     return S, T
 
 
@@ -239,8 +247,7 @@
             W[k, where, :] = (product * weight).astype(BF16)
             return carry
         lax.fori_loop(0, 2, rows, 0)
-        if k == 0:
-            send_leads(0)
+        send_leads(k)
         for r in range(4):
             out = lax.dot_general(W[k, :, r * 128:(r + 1) * 128], W[k, :, r * 128:], (((0,), (0,)), ((), ())), preferred_element_type=F32)
             for c in range(r, 4):
@@ -250,7 +257,6 @@
             if k == 1 and r == 1:
                 send(g0.at[pl.ds(pl.multiple_of(other * 320, 64), 320), :], r0c, s_core.at[0], r_core.at[0], at(cc=other))
     send(g1.at[pl.ds(pl.multiple_of(other * 320, 64), 320), :], r1c, s_core.at[1], r_core.at[1], at(cc=other))
-    send_leads(1)
     arrived(r0c, s_core.at[0], r_core.at[0], at(cc=other))
     s0[...] = g0[pl.ds(pl.multiple_of(core * 320, 64), 320), :] + r0c[...]
     for d, to, _ in zs:

time: 120 us -> 120 us (level)
  no operation moved by 1% of the time
where the time goes in v4:
time: 120 us
  Pallas kernels  118 us (98%)
  between operations  1.28 us (1%)
    pallas_call x1, Pallas kernels, fused(): pl.pallas_call(fused_kernel, out_shape=tuple((jax.ShapeDtypeStruct(*o) fo...  116 us

profile of v4, /device:TPU:1, one launch (start us, length us, event | category | flops | bytes accessed | tf_op | source)
XLA Modules:
  0.0 119.6 jit_solution(15579150994315997231)
XLA Ops:
  1.3 116.1 %fused.1 = (bf16[128,8,256]{2,1,0:T(8,128)(2,1)}, f32[512,512]{1,0:T(8,128)}) custom-call(bf16[8,128,1024]{2,1,0:T(8,128)(2,1)} %ops.1, bf16[8,1024,128]{2,1,0:T(8,128)(2,1)} %exc.1, f32[8]{0:T(128)} %scale_hbm.1, s32[1]{0:T(128)S(6)} %copy.7.live_hbm, s32[8,16]{1,0:T(8,128)} %ports_hbm.1), custom_call_target="tpu_custom_call" | custom-call | tf_op jit(solution)/shard_map/fused/pallas_call | solution.py:449
  117.3 2.2 %hand_over.1 = (bf16[128,8,256]{2,1,0:T(8,128)(2,1)}, f32[512,512]{1,0:T(8,128)}) custom-call(bf16[128,8,256]{2,1,0:T(8,128)(2,1)} %get-tuple-element.4.basis_in, f32[512,512]{1,0:T(8,128)} %get-tuple-element.5.upper_in), custom_call_target="tpu_custom_call" | custom-call | tf_op jit(solution)/shard_map/hand_over/pallas_call | solution.py:103
